TPU v7x, 512 devices: a whole 4x8x8 slice. The times are simulated.
512 devices in a mesh: azi: 32 (over x, z), axl: 16 (over y, core).
Axes of the slice: x: 4, y: 8, z: 8, core: 2. Of those that a mesh axis runs over, the one named last changes fastest.
Arguments:
- explicit_residual: float32 [5, 512, 64, 128], P(None, 'azi', 'axl'), may hold values from -400 to 400
- diffusion: float32 [3, 512, 64, 128], P(None, 'azi', 'axl'), may hold values from 100 to 10000
- source_rate: float32 [512, 64, 128], P('azi', 'axl'), may hold values from 0.05 to 1
- line_mats: float32 [3, 2, 5, 5], replicated, may hold values from -0.15 to 1.5
Outputs:
- increment: float32 [5, 512, 64, 128], P(None, 'azi', 'axl')
All inputs are finite; a program needn't handle non-finite values.
Results may differ from a plain program's by a relative error of at most 0.0003.
Values sent between devices are 32-bit elements; how exact they have to be, the bound alone decides.
A program may use at most 64 MiB of HBM per device.

v0:
```python
import functools

import jax
import jax.numpy as jnp
from jax import lax
from jax.experimental import pallas as pl
from jax.experimental.pallas import tpu as pltpu
from jax.sharding import PartitionSpec as P

N = 5
LOWER, UPPER, RIGHT, DIAG = 0, 5, 10, 11


def lane_index():
    return lax.broadcasted_iota(jnp.int32, (8, 128), 1)


def sub_index():
    return lax.broadcasted_iota(jnp.int32, (8, 128), 0)


def roll(x, shift, axis):
    size = 8 if axis == 0 else 128
    return pltpu.roll(x, shift % size, axis)


def azi_from(x, d):
    if abs(d) >= 8:
        return roll(x, -d // 8, 0)
    moved = roll(x, -16 * d, 1)
    if d > 0:
        return jnp.where(lane_index() >= 128 - 16 * d, roll(moved, -1, 0), moved)
    return jnp.where(lane_index() < -16 * d, roll(moved, 1, 0), moved)


def axl_from(x, d):
    return roll(x, -d, 0)


def rad_from(x, d):
    if abs(d) >= 8:
        return roll(x, 64, 1)
    moved = roll(x, -d, 0)
    crossed = sub_index() >= 8 - d if d > 0 else sub_index() < -d
    return jnp.where(crossed, roll(moved, 64, 1), moved)


def factor(m):
    m = [list(row) for row in m]
    inv = []
    for k in range(N):
        inv.append(1.0 / m[k][k])
        for i in range(k + 1, N):
            m[i][k] = m[i][k] * inv[k]
            for j in range(k + 1, N):
                m[i][j] = m[i][j] - m[i][k] * m[k][j]
    return m, inv


def factored_solve(m, inv, b):
    b = list(b)
    for i in range(N):
        for j in range(i):
            b[i] = b[i] - m[i][j] * b[j]
    for i in reversed(range(N)):
        for j in range(i + 1, N):
            b[i] = b[i] - m[i][j] * b[j]
        b[i] = b[i] * inv[i]
    return b


def times(m, v):
    out = []
    for i in range(N):
        acc = m[i][0] * v[0]
        for j in range(1, N):
            acc = acc + m[i][j] * v[j]
        out.append(acc)
    return out


def add(a, b):
    return [x + y for x, y in zip(a, b)]


def sub(a, b):
    return [x - y for x, y in zip(a, b)]


def solve_lines(fields, mats, direction, hats, rows, face, out, neighbour, shifts, first, last):
    base = direction * 50
    convection = [[mats[base + 5 * i + j] for j in range(N)] for i in range(N)]
    reaction = [[mats[base + 25 + 5 * i + j] for j in range(N)] for i in range(N)]
    plus = [[convection[i][j] + (1.0 if i == j else 0.0) for j in range(N)] for i in range(N)]
    minus = [[(1.0 if i == j else 0.0) - convection[i][j] for j in range(N)] for i in range(N)]

    before = neighbour(fields[5, 7], -1)
    after = neighbour(fields[5, 0], 1)
    if first is not None:
        before = jnp.where(first, 0.0, before)
        after = jnp.where(last, 0.0, after)
    face[0] = 0.5 * (before + fields[5, 0])
    face[8] = 0.5 * (fields[5, 7] + after)
    for r in range(1, 8):
        face[r] = 0.5 * (fields[5, r - 1] + fields[5, r])

    def build(r):
        face_lo, face_hi, source = face[r], face[r + 1], fields[6, r]
        middle = 1.0 + face_lo + face_hi
        link_lo, link_hi = face_lo, face_hi
        if first is not None:
            link_lo = jnp.where(first & (r == 0), 0.0, link_lo)
            link_hi = jnp.where(last & (r == 7), 0.0, link_hi)
        diag = [
            [source * reaction[i][j] + middle if i == j else source * reaction[i][j] for j in range(N)]
            for i in range(N)
        ]
        lower = [[link_lo * plus[i][j] for j in range(N)] for i in range(N)]
        upper = [[link_hi * minus[i][j] for j in range(N)] for i in range(N)]
        return diag, lower, upper, [fields[i, r] for i in range(N)]

    def hat(r, col):
        return [hats[r, col * N + i] for i in range(N)]

    def row_matrix(r, start):
        cols = [[rows[r, (start + j) * N + i] for i in range(N)] for j in range(N)]
        return [[cols[j][i] for j in range(N)] for i in range(N)]

    def put(ref, r, col, values):
        for i in range(N):
            ref[r, col * N + i] = values[i]

    def normalise_built(r):
        diag, lower, upper, right = build(r)
        m, inv = factor(diag)
        for j in range(N):
            put(hats, r, LOWER + j, factored_solve(m, inv, [lower[i][j] for i in range(N)]))
            put(hats, r, UPPER + j, factored_solve(m, inv, [upper[i][j] for i in range(N)]))
        put(hats, r, RIGHT, factored_solve(m, inv, right))

    def normalise(r):
        m, inv = factor(row_matrix(r, DIAG))
        for col in range(11):
            put(hats, r, col, factored_solve(m, inv, [rows[r, col * N + i] for i in range(N)]))

    def combine(r, diag, lower, upper, right, prev, following, want_links=True):
        acc = []
        for j in range(N):
            if want_links:
                put(rows, r, LOWER + j, times(lower, prev(LOWER + j)))
            acc.append(sub([diag[i][j] for i in range(N)], times(lower, prev(UPPER + j))))
        total = add(right, times(lower, prev(RIGHT)))
        for j in range(N):
            if want_links:
                put(rows, r, UPPER + j, times(upper, following(UPPER + j)))
            put(rows, r, DIAG + j, sub(acc[j], times(upper, following(LOWER + j))))
        put(rows, r, RIGHT, add(total, times(upper, following(RIGHT))))

    def combine_rows(r, below, above):
        combine(
            r, row_matrix(r, DIAG), row_matrix(r, LOWER), row_matrix(r, UPPER),
            [rows[r, RIGHT * N + i] for i in range(N)],
            lambda col: hat(below, col), lambda col: hat(above, col),
        )

    def borrow(slot, r):
        def one(q, _):
            hats[slot, q] = neighbour(hats[r, q], 1)
            return 0

        lax.fori_loop(0, 11 * N, one, 0, unroll=11)

    @pl.loop(0, 4)
    def _(k):
        normalise_built(2 * k)

    borrow(8, 0)

    @pl.loop(0, 4)
    def _(k):
        r = 2 * k + 1
        combine(r, *build(r), lambda col: hat(r - 1, col), lambda col: hat(r + 1, col))

    @pl.loop(0, 2)
    def _(k):
        normalise(4 * k + 1)

    borrow(9, 1)

    @pl.loop(0, 2)
    def _(k):
        combine_rows(4 * k + 3, 4 * k + 1, 4 * k + 5)

    normalise(3)
    borrow(11, 3)
    combine_rows(7, 3, 11)

    for d in shifts:
        normalise(7)
        combine(
            7, row_matrix(7, DIAG), row_matrix(7, LOWER), row_matrix(7, UPPER),
            [rows[7, RIGHT * N + i] for i in range(N)],
            lambda col: [neighbour(v, -d) for v in hat(7, col)],
            lambda col: [neighbour(v, d) for v in hat(7, col)],
            want_links=first is None or d != shifts[-1],
        )

    diag = row_matrix(7, DIAG)
    if first is None:
        lower, upper = row_matrix(7, LOWER), row_matrix(7, UPPER)
        diag = [[diag[i][j] - lower[i][j] - upper[i][j] for j in range(N)] for i in range(N)]
    m, inv = factor(diag)
    x7 = factored_solve(m, inv, [rows[7, RIGHT * N + i] for i in range(N)])

    def settle(r, below, above):
        lower = [[hats[r, (LOWER + j) * N + i] for j in range(N)] for i in range(N)]
        upper = [[hats[r, (UPPER + j) * N + i] for j in range(N)] for i in range(N)]
        x = add(add(hat(r, RIGHT), times(lower, below)), times(upper, above))
        for i in range(N):
            out[i, r] = x[i]
        return x

    for i in range(N):
        out[i, 7] = x7[i]
    x_low = [neighbour(v, -1) for v in x7]
    x3 = settle(3, x_low, x7)
    x1 = settle(1, x_low, x3)
    x5 = settle(5, x3, x7)
    settle(0, x_low, x1)
    settle(2, x1, x3)
    settle(4, x3, x5)
    settle(6, x5, x7)


def azimuthal_kernel(mats, fields, out, hats, rows, face):
    solve_lines(
        fields, mats, 0, hats, rows, face, out, azi_from, (1, 2, 4, 8, 16, 32), None, None
    )


def plane_kernel(mats, right, coeffs, out, fields, mid, planes, hats, rows, face):
    for i in range(N):
        fields[i] = right[i]
    fields[5] = coeffs[0]
    fields[6] = coeffs[2]
    solve_lines(
        fields, mats, 1, hats, rows, face, mid, axl_from, (1, 2, 4),
        sub_index() == 0, sub_index() == 7,
    )

    def turned(plane):
        flat = plane.reshape(64, 128).T
        return jnp.concatenate([flat[:64], flat[64:]], axis=1)

    for i in range(N):
        planes[i] = turned(mid[i])
    planes[5] = turned(coeffs[1])
    planes[6] = turned(coeffs[2])
    for i in range(7):
        for r in range(8):
            fields[i, r] = planes[i, pl.ds(r, 8, stride=8), :]
    low_half = lane_index() < 64
    solve_lines(
        fields, mats, 2, hats, rows, face, mid, rad_from, (1, 2, 4, 8),
        (sub_index() == 0) & low_half, (sub_index() == 7) & jnp.logical_not(low_half),
    )
    for i in range(N):
        for r in range(8):
            planes[i, pl.ds(r, 8, stride=8), :] = mid[i, r]
        both = planes[i]
        out[i] = jnp.concatenate([both[:, :64], both[:, 64:]], axis=0).T.reshape(8, 8, 128)


SOLVER_SCRATCH = [
    pltpu.VMEM((12, 55, 8, 128), jnp.float32),
    pltpu.VMEM((8, 80, 8, 128), jnp.float32),
    pltpu.VMEM((9, 8, 128), jnp.float32),
]
IN_VMEM = pl.BlockSpec(memory_space=pltpu.VMEM)
IN_SMEM = pl.BlockSpec(memory_space=pltpu.SMEM)
LIMITS = pltpu.CompilerParams(vmem_limit_bytes=32 * 1024 * 1024)


def solve_azimuthal(mats, fields):
    return pl.pallas_call(
        azimuthal_kernel,
        out_shape=jax.ShapeDtypeStruct((5, 8, 8, 128), jnp.float32),
        in_specs=[IN_SMEM, IN_VMEM],
        out_specs=IN_VMEM,
        scratch_shapes=SOLVER_SCRATCH,
        compiler_params=LIMITS,
        cost_estimate=pl.CostEstimate(flops=40000000, bytes_accessed=400000, transcendentals=0),
    )(mats, fields)


def solve_plane(mats, right, coeffs):
    return pl.pallas_call(
        plane_kernel,
        out_shape=jax.ShapeDtypeStruct((5, 8, 8, 128), jnp.float32),
        in_specs=[IN_SMEM, IN_VMEM, IN_VMEM],
        out_specs=IN_VMEM,
        scratch_shapes=[
            pltpu.VMEM((7, 8, 8, 128), jnp.float32),
            pltpu.VMEM((5, 8, 8, 128), jnp.float32),
            pltpu.VMEM((7, 64, 128), jnp.float32),
        ]
        + SOLVER_SCRATCH,
        compiler_params=LIMITS,
        cost_estimate=pl.CostEstimate(flops=80000000, bytes_accessed=500000, transcendentals=0),
    )(mats, right, coeffs)


def to_plane(block):
    q = block.shape[1]
    moved = lax.all_to_all(block.reshape(16, q * 4, 128), "axl", 0, 0, tiled=True)
    return moved.reshape(8, 2, q, 4, 128).transpose(2, 1, 3, 0, 4).reshape(q, 8, 8, 128)


def from_plane(plane):
    moved = plane.reshape(5, 2, 4, 8, 128).transpose(3, 1, 0, 2, 4).reshape(16, 20, 128)
    moved = lax.all_to_all(moved, "axl", 0, 0, tiled=True)
    return moved.reshape(16, 5, 4, 128).transpose(1, 0, 2, 3)


def body(explicit_residual, diffusion, source_rate, line_mats):
    mats = line_mats.reshape(150)
    coeffs = jnp.stack([diffusion[1], diffusion[2], source_rate], axis=1)
    plane_coeffs = to_plane(coeffs)
    fields = jnp.concatenate([explicit_residual, diffusion[:1], source_rate[None]], axis=0)
    packed = fields.reshape(7, 2, 8, 32, 16).transpose(3, 0, 2, 1, 4).reshape(32, 14, 128)
    lines = lax.all_to_all(packed, "azi", 0, 0, tiled=True)
    lines = lines.reshape(32, 56, 32).transpose(1, 0, 2).reshape(7, 8, 8, 128)
    first = solve_azimuthal(mats, lines)
    packed = first.reshape(40, 32, 32).transpose(1, 0, 2).reshape(32, 10, 128)
    packed = lax.all_to_all(packed, "azi", 0, 0, tiled=True)
    block = packed.reshape(32, 5, 8, 2, 16).transpose(3, 2, 1, 0, 4).reshape(16, 5, 4, 128)
    return from_plane(solve_plane(mats, to_plane(block), plane_coeffs))


def solution(mesh):
    in_specs = (
        P(None, "azi", "axl", None),
        P(None, "azi", "axl", None),
        P("azi", "axl", None),
        P(),
    )
    out_specs = P(None, "azi", "axl", None)
    return jax.shard_map(body, mesh=mesh, in_specs=in_specs, out_specs=out_specs, check_vma=False)
```

profile of v0, /device:TPU:1, one launch (start us, length us, event | category | flops | bytes accessed | tf_op | source)
XLA Modules:
  0.0 109.3 jit_solution(18017107247582907718)
XLA Ops:
  0.0 0.9 concatenate.12
  0.9 0.8 fusion
  1.7 0.8 concatenate.11
  2.5 1.3 %concatenate.10 = f32[5,2,8,32,16]{4,3,2,1,0:T(8,128)S(1)} reshape(f32[5,16,4,128]{3,2,1,0:T(4,128)} %param.4) | data formatting | bytes 327680 | tf_op jit(solution)/shard_map/concatenate | solution.py:329
  3.9 1.2 %maximum_bitcast_fusion = f32[32,7,8,2,16]{4,0,2,3,1:T(8,128)S(1)} fusion(f32[1,2,8,32,16]{4,3,2,1,0:T(8,128)S(1)} %concatenate.12, f32[1,2,8,32,16]{4,3,2,1,0:T(8,128)} %concatenate.11, f32[5,2,8,32,16]{4,3,2,1,0:T(8,128)S(1)} %concatenate.10), kind=kLoop, calls=%fused_computation | loop fusion | flops 114688 | bytes 458752 | tf_op jit(solution)/shard_map/transpose | solution.py:330
  5.1 0.5 copy.21
  5.6 1.0 copy.22
  6.7 13.7 %all-to-all-start = ((f32[32,14,128]{2,1,0:T(8,128)}), f32[32,14,128]{2,1,0:T(8,128)S(1)}, u32[]{:S(2)}, u32[]{:S(2)}) async-start(f32[32,14,128]{2,1,0:T(8,128)} %copy.22), calls=%async_computation | async-start | bytes 524288 | tf_op jit(solution)/shard_map/all_to_all | solution.py:331
  20.4 0.1 reshape.50.mats
  20.5 9.5 %all-to-all-done = f32[32,14,128]{2,1,0:T(8,128)S(1)} async-done(((f32[32,14,128]{2,1,0:T(8,128)}), f32[32,14,128]{2,1,0:T(8,128)S(1)}, u32[]{:S(2)}, u32[]{:S(2)}) %all-to-all-start) | async-done | bytes 229408 | tf_op jit(solution)/shard_map/all_to_all | solution.py:331
  30.1 0.2 reshape.52
  30.3 0.2 copy.23
  30.5 0.2 reshape.53.fields
  30.7 5.6 %shard_map.46 = f32[5,8,8,128]{3,2,1,0:T(8,128)S(1)} custom-call(f32[150]{0:T(256)S(1)} %reshape.50.mats, f32[7,8,8,128]{3,2,1,0:T(8,128)S(1)} %reshape.53.fields), custom_call_target="tpu_custom_call" | custom-call | flops 40000000 | bytes 400000 | tf_op jit(solution)/shard_map/pallas_call | solution.py:285
  36.4 0.2 reshape.54
  36.6 0.4 copy.24
  37.0 0.9 reshape.55
  37.9 6.3 %all-to-all-start.1 = ((f32[32,10,128]{2,1,0:T(8,128)}), f32[32,10,128]{2,1,0:T(8,128)S(1)}, u32[]{:S(2)}, u32[]{:S(2)}) async-start(f32[32,10,128]{2,1,0:T(8,128)} %reshape.55), calls=%async_computation.1 | async-start | bytes 524288 | tf_op jit(solution)/shard_map/all_to_all | solution.py:335
  44.2 0.7 copy.32
  44.9 8.9 %all-to-all-done.1 = f32[32,10,128]{2,1,0:T(8,128)S(1)} async-done(((f32[32,10,128]{2,1,0:T(8,128)}), f32[32,10,128]{2,1,0:T(8,128)S(1)}, u32[]{:S(2)}, u32[]{:S(2)}) %all-to-all-start.1) | async-done | bytes 163872 | tf_op jit(solution)/shard_map/all_to_all | solution.py:335
  53.8 10.7 %all-to-all-start.3 = ((f32[16,12,128]{2,1,0:T(8,128)}), f32[16,12,128]{2,1,0:T(8,128)S(1)}, u32[]{:S(2)}, u32[]{:S(2)}) async-start(f32[16,12,128]{2,1,0:T(8,128)} %copy.32), calls=%async_computation.3 | async-start | bytes 262144 | tf_op jit(solution)/shard_map/all_to_all | solution.py:315
  64.5 0.2 copy.25
  64.8 0.4 copy.26
  65.2 1.0 reshape_reshape.3
  66.3 7.4 %all-to-all-done.3 = f32[16,12,128]{2,1,0:T(8,128)S(1)} async-done(((f32[16,12,128]{2,1,0:T(8,128)}), f32[16,12,128]{2,1,0:T(8,128)S(1)}, u32[]{:S(2)}, u32[]{:S(2)}) %all-to-all-start.3) | async-done | bytes 98336 | tf_op jit(solution)/shard_map/all_to_all | solution.py:315
  73.7 3.6 %all-to-all-start.2 = ((f32[16,20,128]{2,1,0:T(8,128)}), f32[16,20,128]{2,1,0:T(8,128)S(1)}, u32[]{:S(2)}, u32[]{:S(2)}) async-start(f32[16,20,128]{2,1,0:T(8,128)} %reshape_reshape.3), calls=%async_computation.2 | async-start | bytes 393216 | tf_op jit(solution)/shard_map/all_to_all | solution.py:315
  77.4 9.6 %all-to-all-done.2 = f32[16,20,128]{2,1,0:T(8,128)S(1)} async-done(((f32[16,20,128]{2,1,0:T(8,128)}), f32[16,20,128]{2,1,0:T(8,128)S(1)}, u32[]{:S(2)}, u32[]{:S(2)}) %all-to-all-start.2) | async-done | bytes 163872 | tf_op jit(solution)/shard_map/all_to_all | solution.py:315
  87.0 8.2 %shard_map.47 = f32[5,8,8,128]{3,2,1,0:T(8,128)S(1)} custom-call(f32[150]{0:T(256)S(1)} %reshape.50.mats, f32[5,8,8,128]{3,2,1,0:T(8,128)S(1)} %bitcast.35, f32[3,8,8,128]{3,2,1,0:T(8,128)S(1)} %bitcast.37), custom_call_target="tpu_custom_call" | custom-call | flops 80000000 | bytes 500000 | tf_op jit(solution)/shard_map/pallas_call | solution.py:297
  95.3 0.1 copy.35
  95.4 0.1 copy.36
  95.5 13.1 %all_to_all.25 = f32[16,20,128]{2,1,0:T(8,128)S(1)} all-to-all(f32[16,20,128]{2,1,0:T(8,128)S(1)} %copy.36), channel_id=1, replica_groups=mesh['azi'=32,'axl'=16] {'axl'}, dimensions={0} | all-to-all | bytes 327680 | tf_op jit(solution)/shard_map/all_to_all | solution.py:321
  108.6 0.7 copy.38
  (13 shorter events, 0.2 us)
Async XLA Ops:
  5.1 15.3 %copy-start = (f32[16,4,128]{2,1,0:T(4,128)S(1)}, f32[16,4,128]{2,1,0:T(4,128)}, u32[]{:S(2)}) copy-start(f32[16,4,128]{2,1,0:T(4,128)} %param.6) | copy-start | bytes 98308
  5.1 15.3 %copy-start.1 = (f32[3,2,5,5]{3,1,2,0:T(2,128)S(1)}, f32[3,2,5,5]{3,1,2,0:T(2,128)}, u32[]{:S(2)}) copy-start(f32[3,2,5,5]{3,1,2,0:T(2,128)} %param.7) | copy-start | bytes 1804
  6.7 23.4 %all-to-all-start = ((f32[32,14,128]{2,1,0:T(8,128)}), f32[32,14,128]{2,1,0:T(8,128)S(1)}, u32[]{:S(2)}, u32[]{:S(2)}) async-start(f32[32,14,128]{2,1,0:T(8,128)} %copy.22), calls=%async_computation | async-start | bytes 524288 | tf_op jit(solution)/shard_map/all_to_all | solution.py:331
  37.9 16.0 %all-to-all-start.1 = ((f32[32,10,128]{2,1,0:T(8,128)}), f32[32,10,128]{2,1,0:T(8,128)S(1)}, u32[]{:S(2)}, u32[]{:S(2)}) async-start(f32[32,10,128]{2,1,0:T(8,128)} %reshape.55), calls=%async_computation.1 | async-start | bytes 524288 | tf_op jit(solution)/shard_map/all_to_all | solution.py:335
  53.8 19.9 %all-to-all-start.3 = ((f32[16,12,128]{2,1,0:T(8,128)}), f32[16,12,128]{2,1,0:T(8,128)S(1)}, u32[]{:S(2)}, u32[]{:S(2)}) async-start(f32[16,12,128]{2,1,0:T(8,128)} %copy.32), calls=%async_computation.3 | async-start | bytes 262144 | tf_op jit(solution)/shard_map/all_to_all | solution.py:315
  73.7 13.2 %all-to-all-start.2 = ((f32[16,20,128]{2,1,0:T(8,128)}), f32[16,20,128]{2,1,0:T(8,128)S(1)}, u32[]{:S(2)}, u32[]{:S(2)}) async-start(f32[16,20,128]{2,1,0:T(8,128)} %reshape_reshape.3), calls=%async_computation.2 | async-start | bytes 393216 | tf_op jit(solution)/shard_map/all_to_all | solution.py:315
where the time goes:
time: 110 us; the launch traced here: 109 us
  waiting for transfers between devices  35.5 us (32%)
  starting transfers between devices  34.3 us (31%)
  Pallas kernels  13.9 us (13%)
  blocking collectives  13.1 us (12%)
  local copies, waits for them, and re-layouts  11.2 us (10%)
  other arithmetic  1.19 us (1%)
    all_to_all x2, waiting for transfers between devices, to_plane(): lax.all_to_all(block.reshape(16, q * 4, 128), 'axl', 0, 0, tiled=True)  17 us
    all_to_all x2, starting transfers between devices, to_plane(): lax.all_to_all(block.reshape(16, q * 4, 128), 'axl', 0, 0, tiled=True)  14.3 us
    all_to_all x1, starting transfers between devices, body(): lines = lax.all_to_all(packed, 'azi', 0, 0, tiled=True)  13.7 us
    all_to_all x1, blocking collectives, from_plane(): moved = lax.all_to_all(moved, 'axl', 0, 0, tiled=True)  13.1 us
    all_to_all x1, waiting for transfers between devices, body(): lines = lax.all_to_all(packed, 'azi', 0, 0, tiled=True)  9.54 us
    all_to_all x1, waiting for transfers between devices, body(): packed = lax.all_to_all(packed, 'azi', 0, 0, tiled=True)  8.94 us
    pallas_call x1, Pallas kernels, solve_plane(): pl.pallas_call(plane_kernel, out_shape=jax.ShapeDtypeStruct((5, 8, 8, 128...  8.25 us
    all_to_all x1, starting transfers between devices, body(): packed = lax.all_to_all(packed, 'azi', 0, 0, tiled=True)  6.29 us
  transfers between devices with their start and end apart: 4, of which 4 were waited for; matrix products, arithmetic and copies ran while one was open for 2% of the time, Pallas kernels for 0%

commit v1 on v0

--- a/solution.py
+++ b/solution.py
@@ -1,5 +1,3 @@
-import functools
-
 import jax
 import jax.numpy as jnp
 from jax import lax
@@ -25,12 +23,20 @@
 
 
 def azi_from(x, d):
-    if abs(d) >= 8:
-        return roll(x, -d // 8, 0)
-    moved = roll(x, -16 * d, 1)
-    if d > 0:
-        return jnp.where(lane_index() >= 128 - 16 * d, roll(moved, -1, 0), moved)
-    return jnp.where(lane_index() < -16 * d, roll(moved, 1, 0), moved)
+    if abs(d) >= 16:
+        return roll(x, -2 * d, 1)
+    if d == 1:
+        ahead, behind = roll(x, -16, 1), roll(x, 16, 1)
+        carried = jnp.where(sub_index() == 7, roll(ahead, -1, 0), roll(behind, -1, 0))
+        return jnp.where(lane_index() % 32 < 16, ahead, carried)
+    if d == -1:
+        ahead, behind = roll(x, -16, 1), roll(x, 16, 1)
+        carried = jnp.where(sub_index() == 0, roll(behind, 1, 0), roll(ahead, 1, 0))
+        return jnp.where(lane_index() % 32 < 16, carried, behind)
+    e = d // 2
+    moved = roll(x, -e, 0)
+    crossed = sub_index() >= 8 - e if e > 0 else sub_index() < -e
+    return jnp.where(crossed, roll(moved, -32 if e > 0 else 32, 1), moved)
 
 
 def axl_from(x, d):
@@ -232,17 +238,155 @@
     settle(6, x5, x7)
 
 
-def azimuthal_kernel(mats, fields, out, hats, rows, face):
+def swap_blocks(values):
+    values = list(values)
+    count = len(values)
+    width = 128 // count
+    bit = 1
+    while bit < count:
+        upper = (lane_index() // (bit * width)) % 2 == 1
+        for a in range(count):
+            if a & bit == 0:
+                lo, hi = values[a], values[a | bit]
+                values[a] = jnp.where(upper, roll(hi, bit * width, 1), lo)
+                values[a | bit] = jnp.where(upper, hi, roll(lo, -bit * width, 1))
+        bit *= 2
+    return values
+
+
+class Exchange:
+    def __init__(self, axis, count, send, recv, rows, pitch, send_sem, recv_sem):
+        self.axis, self.count, self.rows, self.pitch = axis, count, rows, pitch
+        self.send, self.recv = send, recv
+        self.send_sem, self.recv_sem = send_sem, recv_sem
+        self.me = lax.axis_index(axis)
+
+    def slot(self, ref, device):
+        return ref.at[pl.ds(pl.multiple_of(device * self.pitch, 8), self.rows)]
+
+    def copy(self, k):
+        target = lax.rem(self.me + k, self.count)
+        return pltpu.make_async_remote_copy(
+            src_ref=self.slot(self.send, target),
+            dst_ref=self.slot(self.recv, self.me),
+            send_sem=self.send_sem.at[k],
+            recv_sem=self.recv_sem.at[k],
+            device_id={self.axis: target},
+            device_id_type=pl.DeviceIdType.MESH,
+        )
+
+    def start(self):
+        @pl.loop(1, self.count)
+        def _(k):
+            self.copy(k).start()
+
+        own = pl.ds(pl.multiple_of(self.me * self.pitch, 8), self.rows)
+        self.recv[own, :] = self.send[own, :]
+
+    def wait_recv(self):
+        @pl.loop(1, self.count)
+        def _(k):
+            self.copy(k).wait_recv()
+
+    def wait_send(self):
+        @pl.loop(1, self.count)
+        def _(k):
+            self.copy(k).wait_send()
+
+
+def kernel(
+    mats, explicit, diffusion, source_rate, out,
+    tiles, staged, a_send, a_recv, b_send, b_recv, k_send, k_recv, c_send, c_recv, o_send, o_recv,
+    fields, mid, planes, hats, rows, face, azi_sems, axl_sems,
+):
+    barrier = pltpu.get_barrier_semaphore()
+    for axis, count in (("azi", 32), ("axl", 16)):
+        position = lax.axis_index(axis)
+
+        @pl.loop(1, count)
+        def _(k):
+            pl.semaphore_signal(
+                barrier, inc=1, device_id={axis: lax.rem(position + k, count)},
+                device_id_type=pl.DeviceIdType.MESH,
+            )
+
+    lines_out = Exchange("azi", 32, a_send, a_recv, 14, 16, azi_sems.at[0], azi_sems.at[1])
+    lines_back = Exchange("azi", 32, b_send, b_recv, 10, 16, azi_sems.at[2], azi_sems.at[3])
+    coeffs_out = Exchange("axl", 16, k_send, k_recv, 12, 16, axl_sems.at[0], axl_sems.at[1])
+    plane_out = Exchange("axl", 16, c_send, c_recv, 20, 24, axl_sems.at[2], axl_sems.at[3])
+    plane_back = Exchange("axl", 16, o_send, o_recv, 20, 24, axl_sems.at[4], axl_sems.at[5])
+
+    for f in range(7):
+        for m in range(8):
+            for half in range(2):
+                i = (m % 2) * 8 + half * 4 + m // 2
+                part = explicit[f, i] if f < 5 else diffusion[0, i] if f == 5 else source_rate[i]
+                tiles[f, m, pl.ds(half * 4, 4), :] = part
+
+    @pl.loop(0, 7)
+    def _(f):
+        for b, value in enumerate(swap_blocks([tiles[f, m] for m in range(8)])):
+            staged[b, pl.ds(pl.multiple_of(f * 8, 8), 8), :] = value
+
+    for b in range(8):
+        for j in range(4):
+            a_send[pl.ds((j * 8 + b) * 16, 14), :] = staged[b, pl.ds(j, 14, stride=4), :]
+    for i in range(16):
+        for f, part in enumerate((diffusion[1, i], diffusion[2, i], source_rate[i])):
+            k_send[pl.ds(i * 16 + f * 4, 4), :] = part
+
+    pl.semaphore_wait(barrier, 46)
+    lines_out.start()
+    coeffs_out.start()
+    lines_out.wait_recv()
+
+    for f in range(7):
+        for half in range(2):
+            got = [a_recv[pl.ds(t * 128 + f * 2 + half, 8, stride=16), :] for t in range(4)]
+            for k, value in enumerate(swap_blocks(got)):
+                fields[f, half * 4 + k] = value
+
     solve_lines(
-        fields, mats, 0, hats, rows, face, out, azi_from, (1, 2, 4, 8, 16, 32), None, None
+        fields, mats, 0, hats, rows, face, mid, azi_from, (1, 2, 4, 8, 16, 32), None, None
     )
 
-
-def plane_kernel(mats, right, coeffs, out, fields, mid, planes, hats, rows, face):
-    for i in range(N):
-        fields[i] = right[i]
-    fields[5] = coeffs[0]
-    fields[6] = coeffs[2]
+    for f in range(5):
+        for half in range(2):
+            values = swap_blocks([mid[f, half * 4 + k] for k in range(4)])
+            for t in range(4):
+                b_send[pl.ds(t * 128 + f * 2 + half, 8, stride=16), :] = values[t]
+    lines_back.start()
+    lines_back.wait_recv()
+    for f in range(5):
+        for b in range(8):
+            for half in range(2):
+                tiles[f, b, pl.ds(half * 4, 4), :] = b_recv[
+                    pl.ds(b * 16 + f * 2 + half, 4, stride=128), :
+                ]
+
+    @pl.loop(0, 5)
+    def _(f):
+        for m, value in enumerate(swap_blocks([tiles[f, b] for b in range(8)])):
+            tiles[f, m] = value
+
+    for f in range(5):
+        for m in range(8):
+            for half in range(2):
+                i = (m % 2) * 8 + half * 4 + m // 2
+                c_send[pl.ds(i * 24 + f * 4, 4), :] = tiles[f, m, pl.ds(half * 4, 4), :]
+    plane_out.start()
+
+    def axial_rows(r, f, pitch):
+        return pl.ds((r // 4) * pitch + f * 4 + r % 4, 8, stride=2 * pitch)
+
+    coeffs_out.wait_recv()
+    for r in range(8):
+        fields[5, r] = k_recv[axial_rows(r, 0, 16), :]
+        fields[6, r] = k_recv[axial_rows(r, 2, 16), :]
+    plane_out.wait_recv()
+    for r in range(8):
+        for f in range(5):
+            fields[f, r] = c_recv[axial_rows(r, f, 24), :]
     solve_lines(
         fields, mats, 1, hats, rows, face, mid, axl_from, (1, 2, 4),
         sub_index() == 0, sub_index() == 7,
@@ -252,89 +396,75 @@
         flat = plane.reshape(64, 128).T
         return jnp.concatenate([flat[:64], flat[64:]], axis=1)
 
-    for i in range(N):
-        planes[i] = turned(mid[i])
-    planes[5] = turned(coeffs[1])
-    planes[6] = turned(coeffs[2])
-    for i in range(7):
+    planes[6] = turned(fields[6])
+    for r in range(8):
+        fields[6, r] = k_recv[axial_rows(r, 1, 16), :]
+    planes[5] = turned(fields[6])
+    for f in range(5):
+        planes[f] = turned(mid[f])
+    for f in range(7):
         for r in range(8):
-            fields[i, r] = planes[i, pl.ds(r, 8, stride=8), :]
+            fields[f, r] = planes[f, pl.ds(r, 8, stride=8), :]
     low_half = lane_index() < 64
     solve_lines(
         fields, mats, 2, hats, rows, face, mid, rad_from, (1, 2, 4, 8),
         (sub_index() == 0) & low_half, (sub_index() == 7) & jnp.logical_not(low_half),
     )
-    for i in range(N):
+    for f in range(5):
         for r in range(8):
-            planes[i, pl.ds(r, 8, stride=8), :] = mid[i, r]
-        both = planes[i]
-        out[i] = jnp.concatenate([both[:, :64], both[:, 64:]], axis=0).T.reshape(8, 8, 128)
-
-
-SOLVER_SCRATCH = [
-    pltpu.VMEM((12, 55, 8, 128), jnp.float32),
-    pltpu.VMEM((8, 80, 8, 128), jnp.float32),
-    pltpu.VMEM((9, 8, 128), jnp.float32),
-]
+            planes[f, pl.ds(r, 8, stride=8), :] = mid[f, r]
+        both = planes[f]
+        mid[f] = jnp.concatenate([both[:, :64], both[:, 64:]], axis=0).T.reshape(8, 8, 128)
+        for r in range(8):
+            o_send[axial_rows(r, f, 24), :] = mid[f, r]
+    plane_back.start()
+    plane_back.wait_recv()
+    for f in range(5):
+        for i in range(16):
+            out[f, i] = o_recv[pl.ds(i * 24 + f * 4, 4), :]
+    for exchange in (lines_out, lines_back, coeffs_out, plane_out, plane_back):
+        exchange.wait_send()
+
+
 IN_VMEM = pl.BlockSpec(memory_space=pltpu.VMEM)
 IN_SMEM = pl.BlockSpec(memory_space=pltpu.SMEM)
-LIMITS = pltpu.CompilerParams(vmem_limit_bytes=32 * 1024 * 1024)
-
-
-def solve_azimuthal(mats, fields):
+
+
+def body(explicit_residual, diffusion, source_rate, line_mats):
     return pl.pallas_call(
-        azimuthal_kernel,
-        out_shape=jax.ShapeDtypeStruct((5, 8, 8, 128), jnp.float32),
-        in_specs=[IN_SMEM, IN_VMEM],
-        out_specs=IN_VMEM,
-        scratch_shapes=SOLVER_SCRATCH,
-        compiler_params=LIMITS,
-        cost_estimate=pl.CostEstimate(flops=40000000, bytes_accessed=400000, transcendentals=0),
-    )(mats, fields)
-
-
-def solve_plane(mats, right, coeffs):
-    return pl.pallas_call(
-        plane_kernel,
-        out_shape=jax.ShapeDtypeStruct((5, 8, 8, 128), jnp.float32),
-        in_specs=[IN_SMEM, IN_VMEM, IN_VMEM],
+        kernel,
+        out_shape=jax.ShapeDtypeStruct((5, 16, 4, 128), jnp.float32),
+        in_specs=[IN_SMEM, IN_VMEM, IN_VMEM, IN_VMEM],
         out_specs=IN_VMEM,
         scratch_shapes=[
             pltpu.VMEM((7, 8, 8, 128), jnp.float32),
+            pltpu.VMEM((8, 64, 128), jnp.float32),
+            pltpu.VMEM((512, 128), jnp.float32),
+            pltpu.VMEM((512, 128), jnp.float32),
+            pltpu.VMEM((512, 128), jnp.float32),
+            pltpu.VMEM((512, 128), jnp.float32),
+            pltpu.VMEM((256, 128), jnp.float32),
+            pltpu.VMEM((256, 128), jnp.float32),
+            pltpu.VMEM((384, 128), jnp.float32),
+            pltpu.VMEM((384, 128), jnp.float32),
+            pltpu.VMEM((384, 128), jnp.float32),
+            pltpu.VMEM((384, 128), jnp.float32),
+            pltpu.VMEM((7, 8, 8, 128), jnp.float32),
             pltpu.VMEM((5, 8, 8, 128), jnp.float32),
             pltpu.VMEM((7, 64, 128), jnp.float32),
-        ]
-        + SOLVER_SCRATCH,
-        compiler_params=LIMITS,
-        cost_estimate=pl.CostEstimate(flops=80000000, bytes_accessed=500000, transcendentals=0),
-    )(mats, right, coeffs)
-
-
-def to_plane(block):
-    q = block.shape[1]
-    moved = lax.all_to_all(block.reshape(16, q * 4, 128), "axl", 0, 0, tiled=True)
-    return moved.reshape(8, 2, q, 4, 128).transpose(2, 1, 3, 0, 4).reshape(q, 8, 8, 128)
-
-
-def from_plane(plane):
-    moved = plane.reshape(5, 2, 4, 8, 128).transpose(3, 1, 0, 2, 4).reshape(16, 20, 128)
-    moved = lax.all_to_all(moved, "axl", 0, 0, tiled=True)
-    return moved.reshape(16, 5, 4, 128).transpose(1, 0, 2, 3)
-
-
-def body(explicit_residual, diffusion, source_rate, line_mats):
-    mats = line_mats.reshape(150)
-    coeffs = jnp.stack([diffusion[1], diffusion[2], source_rate], axis=1)
-    plane_coeffs = to_plane(coeffs)
-    fields = jnp.concatenate([explicit_residual, diffusion[:1], source_rate[None]], axis=0)
-    packed = fields.reshape(7, 2, 8, 32, 16).transpose(3, 0, 2, 1, 4).reshape(32, 14, 128)
-    lines = lax.all_to_all(packed, "azi", 0, 0, tiled=True)
-    lines = lines.reshape(32, 56, 32).transpose(1, 0, 2).reshape(7, 8, 8, 128)
-    first = solve_azimuthal(mats, lines)
-    packed = first.reshape(40, 32, 32).transpose(1, 0, 2).reshape(32, 10, 128)
-    packed = lax.all_to_all(packed, "azi", 0, 0, tiled=True)
-    block = packed.reshape(32, 5, 8, 2, 16).transpose(3, 2, 1, 0, 4).reshape(16, 5, 4, 128)
-    return from_plane(solve_plane(mats, to_plane(block), plane_coeffs))
+            pltpu.VMEM((12, 55, 8, 128), jnp.float32),
+            pltpu.VMEM((8, 80, 8, 128), jnp.float32),
+            pltpu.VMEM((9, 8, 128), jnp.float32),
+            pltpu.SemaphoreType.DMA((4, 32)),
+            pltpu.SemaphoreType.DMA((6, 16)),
+        ],
+        compiler_params=pltpu.CompilerParams(
+            collective_id=0, has_side_effects=True, vmem_limit_bytes=32 * 1024 * 1024
+        ),
+        cost_estimate=pl.CostEstimate(
+            flops=120000000, bytes_accessed=600000, transcendentals=0
+        ),
+    )(line_mats.reshape(150), explicit_residual, diffusion, source_rate)
 
 
 def solution(mesh):

time: 110 us -> 64.1 us (0.58)
  Pallas kernels: 13.9 us -> 60.6 us
  waiting for transfers between devices: 35.5 us -> 0 us
  starting transfers between devices: 34.3 us -> 0 us
  blocking collectives: 13.1 us -> 0 us
  local copies, waits for them, and re-layouts: 11.2 us -> 3.3 us
  other arithmetic: 1.19 us -> 0 us
    pallas_call x2 -> x1, Pallas kernels: 13.9 us -> 60.6 us  [body(): pl.pallas_call(kernel, out_shape=jax.ShapeDtypeStruct((5, 16, 4, 128), jn...]
    all_to_all x4 -> x0, waiting for transfers between devices: 35.5 us -> none  [the longest x2 17 us: to_plane(): lax.all_to_all(block.reshape(16, q * 4, 128), 'axl', 0, 0, tiled=True)]
    all_to_all x4 -> x0, starting transfers between devices: 34.3 us -> none  [the longest x2 14.3 us: to_plane(): lax.all_to_all(block.reshape(16, q * 4, 128), 'axl', 0, 0, tiled=True)]
    all_to_all x1 -> x0, blocking collectives: 13.1 us -> none  [from_plane(): moved = lax.all_to_all(moved, 'axl', 0, 0, tiled=True)]
    reshape x9 -> x1, local copies, waits for them, and re-layouts: 3.59 us -> 0.1 us  [body(): line_mats.reshape(150)]
    unnamed x6 -> x8, local copies, waits for them, and re-layouts: 0.02 us -> 3.2 us
    concatenate x3 -> x0, local copies, waits for them, and re-layouts: 3.06 us -> none  [body(): jnp.concatenate([explicit_residual, diffusion[:1], source_rate[None]], ax...]
    transpose x7 -> x0, local copies, waits for them, and re-layouts: 2.27 us -> none  [the longest x1 0.73 us: from_plane(): return moved.reshape(16, 5, 4, 128).transpose(1, 0, 2, 3)]
  transfers between devices with their start and end apart: 4 -> 0, of which waited for: 4 -> 0; matrix products, arithmetic and copies ran while one was open for 2% -> 0% of each run, Pallas kernels for 0% -> 0%
where the time goes in v1:
time: 64.1 us; the launch traced here: 63.9 us
  Pallas kernels  60.6 us (95%)
  local copies, waits for them, and re-layouts  3.3 us (5%)
    pallas_call x1, Pallas kernels, body(): pl.pallas_call(kernel, out_shape=jax.ShapeDtypeStruct((5, 16, 4, 128), jn...  60.6 us
    unnamed x8, local copies, waits for them, and re-layouts  3.2 us

profile of v1, /device:TPU:1, one launch (start us, length us, event | category | flops | bytes accessed | tf_op | source)
XLA Modules:
  0.0 63.9 jit_solution(13495893253433441994)
XLA Ops:
  0.0 0.0 copy-start.2
  0.0 0.7 %copy.5 = f32[3,2,5,5]{3,2,1,0:T(8,128)S(1)} copy(f32[3,2,5,5]{3,1,2,0:T(2,128)} %param.7) | data formatting | bytes 1200 | tf_op args[3]
  0.7 0.1 reshape.3.mats
  0.8 0.0 copy-done.2
  0.8 0.0 copy-start
  0.9 0.9 %copy-done = f32[5,16,4,128]{3,2,1,0:T(4,128)S(1)} copy-done((f32[5,16,4,128]{3,2,1,0:T(4,128)S(1)}, f32[5,16,4,128]{3,2,1,0:T(4,128)}, u32[]{:S(2)}) %copy-start) | copy-done | bytes 163864
  1.8 0.0 copy-start.1
  1.8 0.9 %copy-done.1 = f32[3,16,4,128]{3,2,1,0:T(4,128)S(1)} copy-done((f32[3,16,4,128]{3,2,1,0:T(4,128)S(1)}, f32[3,16,4,128]{3,2,1,0:T(4,128)}, u32[]{:S(2)}) %copy-start.1) | copy-done | bytes 98328
  2.7 60.6 %shard_map.46 = f32[5,16,4,128]{3,2,1,0:T(4,128)S(1)} custom-call(f32[150]{0:T(256)S(1)} %reshape.3.mats, f32[5,16,4,128]{3,2,1,0:T(4,128)S(1)} %copy-done, f32[3,16,4,128]{3,2,1,0:T(4,128)S(1)} %copy-done.1, f32[16,4,128]{2,1,0:T(4,128)S(1)} %copy-done.2), custom_call_target="tpu_custom_call" | custom-call | flops 120000000 | bytes 600000 | tf_op jit(solution)/shard_map/pallas_call | solution.py:434
  63.2 0.7 %copy.7 = f32[5,16,4,128]{3,2,1,0:T(4,128)} copy(f32[5,16,4,128]{3,2,1,0:T(4,128)S(1)} %shard_map.46) | data formatting | bytes 327680
Async XLA Ops:
  0.0 0.8 %copy-start.2 = (f32[16,4,128]{2,1,0:T(4,128)S(1)}, f32[16,4,128]{2,1,0:T(4,128)}, u32[]{:S(2)}) copy-start(f32[16,4,128]{2,1,0:T(4,128)} %source_rate.1) | copy-start | bytes 98308
  0.8 0.9 %copy-start = (f32[5,16,4,128]{3,2,1,0:T(4,128)S(1)}, f32[5,16,4,128]{3,2,1,0:T(4,128)}, u32[]{:S(2)}) copy-start(f32[5,16,4,128]{3,2,1,0:T(4,128)} %explicit.1) | copy-start | bytes 491524
  1.8 0.9 %copy-start.1 = (f32[3,16,4,128]{3,2,1,0:T(4,128)S(1)}, f32[3,16,4,128]{3,2,1,0:T(4,128)}, u32[]{:S(2)}) copy-start(f32[3,16,4,128]{3,2,1,0:T(4,128)} %diffusion.1) | copy-start | bytes 294916

commit v2 on v1

v2 whole, which is shorter than its diff:
```python
import jax
import jax.numpy as jnp
from jax import lax
from jax.experimental import pallas as pl
from jax.experimental.pallas import tpu as pltpu
from jax.sharding import PartitionSpec as P

N = 5
LOWER, UPPER, DIAG = 0, 5, 10


def lane_index():
    return lax.broadcasted_iota(jnp.int32, (8, 128), 1)


def sub_index():
    return lax.broadcasted_iota(jnp.int32, (8, 128), 0)


def roll(x, shift, axis):
    size = 8 if axis == 0 else 128
    return pltpu.roll(x, shift % size, axis)


def azi_from(x, d):
    if abs(d) >= 16:
        return roll(x, -2 * d, 1)
    if d == 1:
        ahead, behind = roll(x, -16, 1), roll(x, 16, 1)
        carried = jnp.where(sub_index() == 7, roll(ahead, -1, 0), roll(behind, -1, 0))
        return jnp.where(lane_index() % 32 < 16, ahead, carried)
    if d == -1:
        ahead, behind = roll(x, -16, 1), roll(x, 16, 1)
        carried = jnp.where(sub_index() == 0, roll(behind, 1, 0), roll(ahead, 1, 0))
        return jnp.where(lane_index() % 32 < 16, carried, behind)
    e = d // 2
    moved = roll(x, -e, 0)
    crossed = sub_index() >= 8 - e if e > 0 else sub_index() < -e
    return jnp.where(crossed, roll(moved, -32 if e > 0 else 32, 1), moved)


def axl_from(x, d):
    return roll(x, -d, 0)


def rad_from(x, d):
    if abs(d) >= 8:
        return roll(x, 64, 1)
    moved = roll(x, -d, 0)
    crossed = sub_index() >= 8 - d if d > 0 else sub_index() < -d
    return jnp.where(crossed, roll(moved, 64, 1), moved)


def factor(m):
    m = [list(row) for row in m]
    inv = []
    for k in range(N):
        inv.append(1.0 / m[k][k])
        for i in range(k + 1, N):
            m[i][k] = m[i][k] * inv[k]
            for j in range(k + 1, N):
                m[i][j] = m[i][j] - m[i][k] * m[k][j]
    return m, inv


def factored_solve(m, inv, b):
    b = list(b)
    for i in range(N):
        for j in range(i):
            b[i] = b[i] - m[i][j] * b[j]
    for i in reversed(range(N)):
        for j in range(i + 1, N):
            b[i] = b[i] - m[i][j] * b[j]
        b[i] = b[i] * inv[i]
    return b


def times(m, v):
    out = []
    for i in range(N):
        acc = m[i][0] * v[0]
        for j in range(1, N):
            acc = acc + m[i][j] * v[j]
        out.append(acc)
    return out


def add(a, b):
    return [x + y for x, y in zip(a, b)]


def sub(a, b):
    return [x - y for x, y in zip(a, b)]


class LineSolver:
    def __init__(self, mats, direction, neighbour, shifts, first, last, store):
        self.hats, self.links, self.factors, self.face = store
        self.neighbour, self.shifts, self.first, self.last = neighbour, shifts, first, last
        base = direction * 50
        convection = [[mats[base + 5 * i + j] for j in range(N)] for i in range(N)]
        self.reaction = [[mats[base + 25 + 5 * i + j] for j in range(N)] for i in range(N)]
        unit = [[1.0 if i == j else 0.0 for j in range(N)] for i in range(N)]
        self.plus = [[unit[i][j] + convection[i][j] for j in range(N)] for i in range(N)]
        self.minus = [[unit[i][j] - convection[i][j] for j in range(N)] for i in range(N)]

    def built_links(self, r):
        link_lo, link_hi = self.face[r], self.face[r + 1]
        if self.first is not None:
            link_lo = jnp.where(self.first & (r == 0), 0.0, link_lo)
            link_hi = jnp.where(self.last & (r == 7), 0.0, link_hi)
        lower = [[link_lo * self.plus[i][j] for j in range(N)] for i in range(N)]
        upper = [[link_hi * self.minus[i][j] for j in range(N)] for i in range(N)]
        return lower, upper

    def built_diag(self, r, source):
        middle = 1.0 + self.face[r] + self.face[r + 1]
        return [
            [
                source * self.reaction[i][j] + middle if i == j else source * self.reaction[i][j]
                for j in range(N)
            ]
            for i in range(N)
        ]

    def matrix(self, ref, slot, start):
        cols = [[ref[slot, (start + j) * N + i] for i in range(N)] for j in range(N)]
        return [[cols[j][i] for j in range(N)] for i in range(N)]

    def put(self, ref, slot, col, values):
        for i in range(N):
            ref[slot, col * N + i] = values[i]

    def keep_factor(self, slot, diag):
        m, inv = factor(diag)
        for i in range(N):
            for j in range(N):
                self.factors[slot, i * N + j] = inv[i] if i == j else m[i][j]
        return m, inv

    def solved(self, slot, right):
        m = [[self.factors[slot, i * N + j] for j in range(N)] for i in range(N)]
        return factored_solve(m, [m[i][i] for i in range(N)], right)

    def hat_column(self, slot, col):
        return [self.hats[slot, col * N + i] for i in range(N)]

    def prepare(self, coeff, source):
        neighbour, face, first = self.neighbour, self.face, self.first
        hats, links = self.hats, self.links
        before, after = neighbour(coeff[7], -1), neighbour(coeff[0], 1)
        if first is not None:
            before = jnp.where(first, 0.0, before)
            after = jnp.where(self.last, 0.0, after)
        face[0] = 0.5 * (before + coeff[0])
        face[8] = 0.5 * (coeff[7] + after)
        for r in range(1, 8):
            face[r] = 0.5 * (coeff[r - 1] + coeff[r])

        def normalise(slot, kept, diag, column):
            m, inv = self.keep_factor(kept, diag)
            for col in range(10):
                self.put(hats, slot, col, factored_solve(m, inv, column(col)))

        def normalise_built(r, kept):
            lower, upper = self.built_links(r)
            both = [lower, upper]
            normalise(
                r, kept, self.built_diag(r, source[r]),
                lambda col: [both[col // N][i][col % N] for i in range(N)],
            )

        def normalise_kept(slot, row, kept):
            normalise(
                slot, kept, self.matrix(links, row, DIAG),
                lambda col: [links[row, col * N + i] for i in range(N)],
            )

        def combine(target, diag, lower, upper, prev, following, want_links=True):
            acc = []
            for j in range(N):
                if want_links:
                    self.put(links, target, LOWER + j, times(lower, prev(LOWER + j)))
                acc.append(sub([diag[i][j] for i in range(N)], times(lower, prev(UPPER + j))))
            for j in range(N):
                if want_links:
                    self.put(links, target, UPPER + j, times(upper, following(UPPER + j)))
                self.put(
                    links, target, DIAG + j, sub(acc[j], times(upper, following(LOWER + j)))
                )

        def combine_kept(target, row, below, above):
            combine(
                target, self.matrix(links, row, DIAG), self.matrix(links, row, LOWER),
                self.matrix(links, row, UPPER), lambda col: self.hat_column(below, col),
                lambda col: self.hat_column(above, col),
            )

        def borrow(slot, r):
            def one(q, _):
                hats[slot, q] = neighbour(hats[r, q], 1)
                return 0

            lax.fori_loop(0, 10 * N, one, 0, unroll=10)

        @pl.loop(0, 4)
        def _(k):
            normalise_built(2 * k, k)

        borrow(8, 0)

        @pl.loop(0, 4)
        def _(k):
            r = 2 * k + 1
            lower, upper = self.built_links(r)
            combine(
                r, self.built_diag(r, source[r]), lower, upper,
                lambda col: self.hat_column(r - 1, col), lambda col: self.hat_column(r + 1, col),
            )

        @pl.loop(0, 2)
        def _(k):
            normalise_kept(4 * k + 1, 4 * k + 1, 4 + k)

        borrow(9, 1)

        @pl.loop(0, 2)
        def _(k):
            combine_kept(8 + k, 4 * k + 3, 4 * k + 1, 4 * k + 5)

        normalise_kept(3, 8, 6)
        borrow(11, 3)
        combine_kept(10, 9, 3, 11)
        for k, d in enumerate(self.shifts):
            row = 10 + k
            normalise_kept(7, row, 7 + k)
            combine(
                row + 1, self.matrix(links, row, DIAG), self.matrix(links, row, LOWER),
                self.matrix(links, row, UPPER),
                lambda col: [neighbour(v, -d) for v in self.hat_column(7, col)],
                lambda col: [neighbour(v, d) for v in self.hat_column(7, col)],
                want_links=first is None or d != self.shifts[-1],
            )
        row = 10 + len(self.shifts)
        diag = self.matrix(links, row, DIAG)
        if first is None:
            lower, upper = self.matrix(links, row, LOWER), self.matrix(links, row, UPPER)
            diag = [[diag[i][j] - lower[i][j] - upper[i][j] for j in range(N)] for i in range(N)]
        self.keep_factor(7 + len(self.shifts), diag)

    def finish(self, right, out):
        neighbour, links = self.neighbour, self.links

        def gather(r, lower, upper, below, above):
            return add(add(r, times(lower, below)), times(upper, above))

        def kept(row):
            return self.matrix(links, row, LOWER), self.matrix(links, row, UPPER)

        def shifted(values, d):
            return [neighbour(v, d) for v in values]

        def load(r):
            return [right[i, r] for i in range(N)]

        hat = {r: self.solved(r // 2, load(r)) for r in (0, 2, 4, 6)}
        hat[8] = shifted(hat[0], 1)
        rhs = {
            r: gather(load(r), *self.built_links(r), hat[r - 1], hat[r + 1]) for r in (1, 3, 5, 7)
        }
        hat[1], hat[5] = self.solved(4, rhs[1]), self.solved(5, rhs[5])
        rhs[3] = gather(rhs[3], *kept(3), hat[1], hat[5])
        rhs[7] = gather(rhs[7], *kept(7), hat[5], shifted(hat[1], 1))
        hat[3] = self.solved(6, rhs[3])
        last = gather(rhs[7], *kept(9), hat[3], shifted(hat[3], 1))
        for k, d in enumerate(self.shifts):
            part = self.solved(7 + k, last)
            last = gather(last, *kept(10 + k), shifted(part, -d), shifted(part, d))
        x = {7: self.solved(7 + len(self.shifts), last)}
        x[-1] = shifted(x[7], -1)

        def settle(r, step):
            lower = self.matrix(self.hats, r, LOWER)
            upper = self.matrix(self.hats, r, UPPER)
            x[r] = gather(hat[r], lower, upper, x[r - step], x[r + step])

        for r, step in ((3, 4), (1, 2), (5, 2), (0, 1), (2, 1), (4, 1), (6, 1)):
            settle(r, step)
        for r in range(8):
            for i in range(N):
                out[i, r] = x[r][i]


def swap_blocks(values):
    values = list(values)
    count = len(values)
    width = 128 // count
    bit = 1
    while bit < count:
        upper = (lane_index() // (bit * width)) % 2 == 1
        for a in range(count):
            if a & bit == 0:
                lo, hi = values[a], values[a | bit]
                values[a] = jnp.where(upper, roll(hi, bit * width, 1), lo)
                values[a | bit] = jnp.where(upper, hi, roll(lo, -bit * width, 1))
        bit *= 2
    return values


class Exchange:
    def __init__(self, axis, count, send, recv, start, rows, pitch, send_sem, recv_sem):
        self.axis, self.count, self.offset = axis, count, start
        self.rows, self.pitch = rows, pitch
        self.send, self.recv = send, recv
        self.send_sem, self.recv_sem = send_sem, recv_sem
        self.me = lax.axis_index(axis)

    def slot(self, ref, device):
        return ref.at[pl.ds(pl.multiple_of(device * self.pitch + self.offset, 8), self.rows)]

    def copy(self, k):
        target = lax.rem(self.me + k, self.count)
        return pltpu.make_async_remote_copy(
            src_ref=self.slot(self.send, target),
            dst_ref=self.slot(self.recv, self.me),
            send_sem=self.send_sem.at[k],
            recv_sem=self.recv_sem.at[k],
            device_id={self.axis: target},
            device_id_type=pl.DeviceIdType.MESH,
        )

    def start(self):
        @pl.loop(1, self.count)
        def _(k):
            self.copy(k).start()

        own = pl.ds(pl.multiple_of(self.me * self.pitch + self.offset, 8), self.rows)
        self.recv[own, :] = self.send[own, :]

    def wait_recv(self):
        @pl.loop(1, self.count)
        def _(k):
            self.copy(k).wait_recv()

    def wait_send(self):
        @pl.loop(1, self.count)
        def _(k):
            self.copy(k).wait_send()


def kernel(
    mats, explicit, diffusion, source_rate, out,
    tiles, staged, a_send, a_recv, b_send, b_recv, k_send, k_recv, c_send, c_recv, o_send, o_recv,
    fields, mid, planes, hats, links, factors, face, azi_sems, axl_sems,
):
    barrier = pltpu.get_barrier_semaphore()
    for axis, count in (("azi", 32), ("axl", 16)):
        position = lax.axis_index(axis)

        @pl.loop(1, count)
        def _(k):
            pl.semaphore_signal(
                barrier, inc=1, device_id={axis: lax.rem(position + k, count)},
                device_id_type=pl.DeviceIdType.MESH,
            )

    lines_coeffs = Exchange("azi", 32, a_send, a_recv, 0, 4, 24, azi_sems.at[4], azi_sems.at[5])
    lines_out = Exchange("azi", 32, a_send, a_recv, 8, 10, 24, azi_sems.at[0], azi_sems.at[1])
    lines_back = Exchange("azi", 32, b_send, b_recv, 0, 10, 16, azi_sems.at[2], azi_sems.at[3])
    coeffs_out = Exchange("axl", 16, k_send, k_recv, 0, 12, 16, axl_sems.at[0], axl_sems.at[1])
    plane_out = Exchange("axl", 16, c_send, c_recv, 0, 20, 24, axl_sems.at[2], axl_sems.at[3])
    plane_back = Exchange("axl", 16, o_send, o_recv, 0, 20, 24, axl_sems.at[4], axl_sems.at[5])

    low_half = lane_index() < 64

    def store(k):
        return hats.at[k], links.at[k], factors.at[k], face.at[k]

    azimuthal = LineSolver(mats, 0, azi_from, (1, 2, 4, 8, 16, 32), None, None, store(0))
    axial = LineSolver(
        mats, 1, axl_from, (1, 2, 4), sub_index() == 0, sub_index() == 7, store(1)
    )
    radial = LineSolver(
        mats, 2, rad_from, (1, 2, 4, 8), (sub_index() == 0) & low_half,
        (sub_index() == 7) & jnp.logical_not(low_half), store(0),
    )

    def stage(f, place, part):
        for m in range(8):
            for half in range(2):
                i = (m % 2) * 8 + half * 4 + m // 2
                tiles[f, m, pl.ds(half * 4, 4), :] = part(i)
        for b, value in enumerate(swap_blocks([tiles[f, m] for m in range(8)])):
            staged[b, pl.ds(place, 8), :] = value

    stage(5, 0, lambda i: diffusion[0, i])
    stage(6, 8, lambda i: source_rate[i])
    for b in range(8):
        for j in range(4):
            a_send[pl.ds((j * 8 + b) * 24, 4), :] = staged[b, pl.ds(j, 4, stride=4), :]

    pl.semaphore_wait(barrier, 46)
    lines_coeffs.start()

    for f in range(5):
        stage(f, 16 + f * 8, lambda i: explicit[f, i])
    for b in range(8):
        for j in range(4):
            a_send[pl.ds((j * 8 + b) * 24 + 8, 10), :] = staged[b, pl.ds(16 + j, 10, stride=4), :]
    lines_out.start()

    for i in range(16):
        for f, part in enumerate((diffusion[1, i], diffusion[2, i], source_rate[i])):
            k_send[pl.ds(i * 16 + f * 4, 4), :] = part
    coeffs_out.start()

    def take_lines(f, row):
        for half in range(2):
            got = [a_recv[pl.ds(t * 192 + row + half, 8, stride=24), :] for t in range(4)]
            for k, value in enumerate(swap_blocks(got)):
                fields[f, half * 4 + k] = value

    lines_coeffs.wait_recv()
    take_lines(5, 0)
    take_lines(6, 2)
    azimuthal.prepare(fields.at[5], fields.at[6])
    lines_out.wait_recv()
    for f in range(5):
        take_lines(f, 8 + 2 * f)
    azimuthal.finish(fields, mid)

    for f in range(5):
        for half in range(2):
            values = swap_blocks([mid[f, half * 4 + k] for k in range(4)])
            for t in range(4):
                b_send[pl.ds(t * 128 + f * 2 + half, 8, stride=16), :] = values[t]
    lines_back.start()

    def axial_rows(r, f, pitch):
        return pl.ds((r // 4) * pitch + f * 4 + r % 4, 8, stride=2 * pitch)

    coeffs_out.wait_recv()
    for r in range(8):
        fields[5, r] = k_recv[axial_rows(r, 0, 16), :]
        fields[6, r] = k_recv[axial_rows(r, 2, 16), :]
    axial.prepare(fields.at[5], fields.at[6])

    lines_back.wait_recv()
    for f in range(5):
        for b in range(8):
            for half in range(2):
                tiles[f, b, pl.ds(half * 4, 4), :] = b_recv[
                    pl.ds(b * 16 + f * 2 + half, 4, stride=128), :
                ]
        for m, value in enumerate(swap_blocks([tiles[f, b] for b in range(8)])):
            tiles[f, m] = value
        for m in range(8):
            for half in range(2):
                i = (m % 2) * 8 + half * 4 + m // 2
                c_send[pl.ds(i * 24 + f * 4, 4), :] = tiles[f, m, pl.ds(half * 4, 4), :]
    plane_out.start()

    def turned(plane):
        flat = plane.reshape(64, 128).T
        return jnp.concatenate([flat[:64], flat[64:]], axis=1)

    def turn_rows(f):
        for r in range(8):
            fields[f, r] = planes[f, pl.ds(r, 8, stride=8), :]

    planes[6] = turned(fields[6])
    for r in range(8):
        fields[5, r] = k_recv[axial_rows(r, 1, 16), :]
    planes[5] = turned(fields[5])
    turn_rows(5)
    turn_rows(6)
    radial.prepare(fields.at[5], fields.at[6])

    plane_out.wait_recv()
    for r in range(8):
        for f in range(5):
            fields[f, r] = c_recv[axial_rows(r, f, 24), :]
    axial.finish(fields, mid)
    for f in range(5):
        planes[f] = turned(mid[f])
        turn_rows(f)
    radial.finish(fields, mid)
    for f in range(5):
        for r in range(8):
            planes[f, pl.ds(r, 8, stride=8), :] = mid[f, r]
        both = planes[f]
        mid[f] = jnp.concatenate([both[:, :64], both[:, 64:]], axis=0).T.reshape(8, 8, 128)
        for r in range(8):
            o_send[axial_rows(r, f, 24), :] = mid[f, r]
    plane_back.start()
    plane_back.wait_recv()
    for f in range(5):
        for i in range(16):
            out[f, i] = o_recv[pl.ds(i * 24 + f * 4, 4), :]
    for exchange in (lines_coeffs, lines_out, lines_back, coeffs_out, plane_out, plane_back):
        exchange.wait_send()


IN_VMEM = pl.BlockSpec(memory_space=pltpu.VMEM)
IN_SMEM = pl.BlockSpec(memory_space=pltpu.SMEM)


def body(explicit_residual, diffusion, source_rate, line_mats):
    return pl.pallas_call(
        kernel,
        out_shape=jax.ShapeDtypeStruct((5, 16, 4, 128), jnp.float32),
        in_specs=[IN_SMEM, IN_VMEM, IN_VMEM, IN_VMEM],
        out_specs=IN_VMEM,
        scratch_shapes=[
            pltpu.VMEM((7, 8, 8, 128), jnp.float32),
            pltpu.VMEM((8, 64, 128), jnp.float32),
            pltpu.VMEM((768, 128), jnp.float32),
            pltpu.VMEM((768, 128), jnp.float32),
            pltpu.VMEM((512, 128), jnp.float32),
            pltpu.VMEM((512, 128), jnp.float32),
            pltpu.VMEM((256, 128), jnp.float32),
            pltpu.VMEM((256, 128), jnp.float32),
            pltpu.VMEM((384, 128), jnp.float32),
            pltpu.VMEM((384, 128), jnp.float32),
            pltpu.VMEM((384, 128), jnp.float32),
            pltpu.VMEM((384, 128), jnp.float32),
            pltpu.VMEM((7, 8, 8, 128), jnp.float32),
            pltpu.VMEM((5, 8, 8, 128), jnp.float32),
            pltpu.VMEM((7, 64, 128), jnp.float32),
            pltpu.VMEM((2, 12, 50, 8, 128), jnp.float32),
            pltpu.VMEM((2, 17, 75, 8, 128), jnp.float32),
            pltpu.VMEM((2, 14, 25, 8, 128), jnp.float32),
            pltpu.VMEM((2, 9, 8, 128), jnp.float32),
            pltpu.SemaphoreType.DMA((6, 32)),
            pltpu.SemaphoreType.DMA((6, 16)),
        ],
        compiler_params=pltpu.CompilerParams(
            collective_id=0, has_side_effects=True, vmem_limit_bytes=32 * 1024 * 1024
        ),
        cost_estimate=pl.CostEstimate(
            flops=120000000, bytes_accessed=600000, transcendentals=0
        ),
    )(line_mats.reshape(150), explicit_residual, diffusion, source_rate)


def solution(mesh):
    in_specs = (
        P(None, "azi", "axl", None),
        P(None, "azi", "axl", None),
        P("azi", "axl", None),
        P(),
    )
    out_specs = P(None, "azi", "axl", None)
    return jax.shard_map(body, mesh=mesh, in_specs=in_specs, out_specs=out_specs, check_vma=False)
```

time: 64.1 us -> 57 us (0.89)
  Pallas kernels: 60.6 us -> 53.5 us
    pallas_call x1, Pallas kernels: 60.6 us -> 53.5 us  [body(): pl.pallas_call(kernel, out_shape=jax.ShapeDtypeStruct((5, 16, 4, 128), jn...]
where the time goes in v2:
time: 57 us; the launch traced here: 56.8 us
  Pallas kernels  53.5 us (94%)
  local copies, waits for them, and re-layouts  3.3 us (6%)
    pallas_call x1, Pallas kernels, body(): pl.pallas_call(kernel, out_shape=jax.ShapeDtypeStruct((5, 16, 4, 128), jn...  53.5 us
    unnamed x8, local copies, waits for them, and re-layouts  3.2 us

profile of v2, /device:TPU:1, one launch (start us, length us, event | category | flops | bytes accessed | tf_op | source)
XLA Modules:
  0.0 56.8 jit_solution(17325007600541982588)
XLA Ops:
  0.0 0.0 copy-start.2
  0.0 0.7 %copy.5 = f32[3,2,5,5]{3,2,1,0:T(8,128)S(1)} copy(f32[3,2,5,5]{3,1,2,0:T(2,128)} %param.7) | data formatting | bytes 1200 | tf_op args[3]
  0.7 0.1 reshape.3.mats
  0.8 0.0 copy-done.2
  0.8 0.0 copy-start
  0.9 0.9 %copy-done = f32[5,16,4,128]{3,2,1,0:T(4,128)S(1)} copy-done((f32[5,16,4,128]{3,2,1,0:T(4,128)S(1)}, f32[5,16,4,128]{3,2,1,0:T(4,128)}, u32[]{:S(2)}) %copy-start) | copy-done | bytes 163864
  1.8 0.0 copy-start.1
  1.8 0.9 %copy-done.1 = f32[3,16,4,128]{3,2,1,0:T(4,128)S(1)} copy-done((f32[3,16,4,128]{3,2,1,0:T(4,128)S(1)}, f32[3,16,4,128]{3,2,1,0:T(4,128)}, u32[]{:S(2)}) %copy-start.1) | copy-done | bytes 98328
  2.7 53.5 %shard_map.46 = f32[5,16,4,128]{3,2,1,0:T(4,128)S(1)} custom-call(f32[150]{0:T(256)S(1)} %reshape.3.mats, f32[5,16,4,128]{3,2,1,0:T(4,128)S(1)} %copy-done, f32[3,16,4,128]{3,2,1,0:T(4,128)S(1)} %copy-done.1, f32[16,4,128]{2,1,0:T(4,128)S(1)} %copy-done.2), custom_call_target="tpu_custom_call" | custom-call | flops 120000000 | bytes 600000 | tf_op jit(solution)/shard_map/pallas_call | solution.py:509
  56.1 0.7 %copy.7 = f32[5,16,4,128]{3,2,1,0:T(4,128)} copy(f32[5,16,4,128]{3,2,1,0:T(4,128)S(1)} %shard_map.46) | data formatting | bytes 327680
Async XLA Ops:
  0.0 0.8 %copy-start.2 = (f32[16,4,128]{2,1,0:T(4,128)S(1)}, f32[16,4,128]{2,1,0:T(4,128)}, u32[]{:S(2)}) copy-start(f32[16,4,128]{2,1,0:T(4,128)} %source_rate.1) | copy-start | bytes 98308
  0.8 0.9 %copy-start = (f32[5,16,4,128]{3,2,1,0:T(4,128)S(1)}, f32[5,16,4,128]{3,2,1,0:T(4,128)}, u32[]{:S(2)}) copy-start(f32[5,16,4,128]{3,2,1,0:T(4,128)} %explicit.1) | copy-start | bytes 491524
  1.8 0.9 %copy-start.1 = (f32[3,16,4,128]{3,2,1,0:T(4,128)S(1)}, f32[3,16,4,128]{3,2,1,0:T(4,128)}, u32[]{:S(2)}) copy-start(f32[3,16,4,128]{3,2,1,0:T(4,128)} %diffusion.1) | copy-start | bytes 294916

commit v3 on v2

--- a/solution.py
+++ b/solution.py
@@ -97,9 +97,8 @@
     def __init__(self, mats, direction, neighbour, shifts, first, last, store):
         self.hats, self.links, self.factors, self.face = store
         self.neighbour, self.shifts, self.first, self.last = neighbour, shifts, first, last
-        base = direction * 50
-        convection = [[mats[base + 5 * i + j] for j in range(N)] for i in range(N)]
-        self.reaction = [[mats[base + 25 + 5 * i + j] for j in range(N)] for i in range(N)]
+        convection = [[mats[direction, i, 0, j] for j in range(N)] for i in range(N)]
+        self.reaction = [[mats[direction, i, 1, j] for j in range(N)] for i in range(N)]
         unit = [[1.0 if i == j else 0.0 for j in range(N)] for i in range(N)]
         self.plus = [[unit[i][j] + convection[i][j] for j in range(N)] for i in range(N)]
         self.minus = [[unit[i][j] - convection[i][j] for j in range(N)] for i in range(N)]
@@ -349,10 +348,20 @@
 
 
 def kernel(
-    mats, explicit, diffusion, source_rate, out,
+    mats, explicit_in, diffusion_in, source_in, out,
+    explicit, diffusion, source_rate,
     tiles, staged, a_send, a_recv, b_send, b_recv, k_send, k_recv, c_send, c_recv, o_send, o_recv,
-    fields, mid, planes, hats, links, factors, face, azi_sems, axl_sems,
+    fields, mid, planes, hats, links, factors, face, load_sems, azi_sems, axl_sems,
 ):
+    loads = [
+        pltpu.make_async_copy(source, target, load_sems.at[n])
+        for n, (source, target) in enumerate(
+            ((diffusion_in, diffusion), (source_in, source_rate), (explicit_in, explicit))
+        )
+    ]
+    for load in loads:
+        load.start()
+
     barrier = pltpu.get_barrier_semaphore()
     for axis, count in (("azi", 32), ("axl", 16)):
         position = lax.axis_index(axis)
@@ -393,6 +402,8 @@
         for b, value in enumerate(swap_blocks([tiles[f, m] for m in range(8)])):
             staged[b, pl.ds(place, 8), :] = value
 
+    loads[0].wait()
+    loads[1].wait()
     stage(5, 0, lambda i: diffusion[0, i])
     stage(6, 8, lambda i: source_rate[i])
     for b in range(8):
@@ -402,6 +413,7 @@
     pl.semaphore_wait(barrier, 46)
     lines_coeffs.start()
 
+    loads[2].wait()
     for f in range(5):
         stage(f, 16 + f * 8, lambda i: explicit[f, i])
     for b in range(8):
@@ -509,9 +521,12 @@
     return pl.pallas_call(
         kernel,
         out_shape=jax.ShapeDtypeStruct((5, 16, 4, 128), jnp.float32),
-        in_specs=[IN_SMEM, IN_VMEM, IN_VMEM, IN_VMEM],
+        in_specs=[IN_SMEM] + [pl.BlockSpec(memory_space=pl.ANY)] * 3,
         out_specs=IN_VMEM,
         scratch_shapes=[
+            pltpu.VMEM((5, 16, 4, 128), jnp.float32),
+            pltpu.VMEM((3, 16, 4, 128), jnp.float32),
+            pltpu.VMEM((16, 4, 128), jnp.float32),
             pltpu.VMEM((7, 8, 8, 128), jnp.float32),
             pltpu.VMEM((8, 64, 128), jnp.float32),
             pltpu.VMEM((768, 128), jnp.float32),
@@ -531,16 +546,17 @@
             pltpu.VMEM((2, 17, 75, 8, 128), jnp.float32),
             pltpu.VMEM((2, 14, 25, 8, 128), jnp.float32),
             pltpu.VMEM((2, 9, 8, 128), jnp.float32),
+            pltpu.SemaphoreType.DMA((3,)),
             pltpu.SemaphoreType.DMA((6, 32)),
             pltpu.SemaphoreType.DMA((6, 16)),
         ],
         compiler_params=pltpu.CompilerParams(
-            collective_id=0, has_side_effects=True, vmem_limit_bytes=32 * 1024 * 1024
+            collective_id=0, has_side_effects=True, vmem_limit_bytes=56 * 1024 * 1024
         ),
         cost_estimate=pl.CostEstimate(
             flops=120000000, bytes_accessed=600000, transcendentals=0
         ),
-    )(line_mats.reshape(150), explicit_residual, diffusion, source_rate)
+    )(line_mats.transpose(0, 2, 1, 3), explicit_residual, diffusion, source_rate)
 
 
 def solution(mesh):

time: 57 us -> 56.3 us (0.988)
  local copies, waits for them, and re-layouts: 3.3 us -> 1.59 us
  Pallas kernels: 53.5 us -> 54.5 us
    unnamed x8 -> x1, local copies, waits for them, and re-layouts: 3.2 us -> 1.59 us
    pallas_call x1, Pallas kernels: 53.5 us -> 54.5 us  [body(): pl.pallas_call(kernel, out_shape=jax.ShapeDtypeStruct((5, 16, 4, 128), jn...]
where the time goes in v3:
time: 56.3 us; the launch traced here: 56.1 us
  Pallas kernels  54.5 us (97%)
  local copies, waits for them, and re-layouts  1.59 us (3%)
    pallas_call x1, Pallas kernels, body(): pl.pallas_call(kernel, out_shape=jax.ShapeDtypeStruct((5, 16, 4, 128), jn...  54.5 us
    unnamed x1, local copies, waits for them, and re-layouts  1.59 us

profile of v3, /device:TPU:1, one launch (start us, length us, event | category | flops | bytes accessed | tf_op | source)
XLA Modules:
  0.0 56.1 jit_solution(7096802465392136701)
XLA Ops:
  0.0 54.5 %shard_map.46 = f32[5,16,4,128]{3,2,1,0:T(4,128)} custom-call(f32[3,5,2,5]{3,2,1,0:T(2,128)} %bitcast.1, f32[5,16,4,128]{3,2,1,0:T(4,128)} %explicit_in.1, f32[3,16,4,128]{3,2,1,0:T(4,128)} %diffusion_in.1, f32[16,4,128]{2,1,0:T(4,128)} %source_in.1), custom_call_target="tpu_custom_call" | custom-call | flops 120000000 | bytes 600000 | tf_op jit(solution)/shard_map/pallas_call | solution.py:521
  54.5 1.6 %copy.6 = f32[5,16,4,128]{3,2,1,0:T(4,128)} copy(f32[5,16,4,128]{3,2,1,0:T(4,128)} %shard_map.46) | data formatting | bytes 327680

commit v4 on v2

--- a/solution.py
+++ b/solution.py
@@ -97,9 +97,8 @@
     def __init__(self, mats, direction, neighbour, shifts, first, last, store):
         self.hats, self.links, self.factors, self.face = store
         self.neighbour, self.shifts, self.first, self.last = neighbour, shifts, first, last
-        base = direction * 50
-        convection = [[mats[base + 5 * i + j] for j in range(N)] for i in range(N)]
-        self.reaction = [[mats[base + 25 + 5 * i + j] for j in range(N)] for i in range(N)]
+        convection = [[mats[direction, i, 0, j] for j in range(N)] for i in range(N)]
+        self.reaction = [[mats[direction, i, 1, j] for j in range(N)] for i in range(N)]
         unit = [[1.0 if i == j else 0.0 for j in range(N)] for i in range(N)]
         self.plus = [[unit[i][j] + convection[i][j] for j in range(N)] for i in range(N)]
         self.minus = [[unit[i][j] - convection[i][j] for j in range(N)] for i in range(N)]
@@ -540,7 +539,7 @@
         cost_estimate=pl.CostEstimate(
             flops=120000000, bytes_accessed=600000, transcendentals=0
         ),
-    )(line_mats.reshape(150), explicit_residual, diffusion, source_rate)
+    )(line_mats.transpose(0, 2, 1, 3), explicit_residual, diffusion, source_rate)
 
 
 def solution(mesh):

time: 57 us -> 57.9 us (1.016)
  local copies, waits for them, and re-layouts: 3.3 us -> 3.95 us
    unnamed x8 -> x9, local copies, waits for them, and re-layouts: 3.2 us -> 3.95 us
where the time goes in v4:
time: 57.9 us; the launch traced here: 57.7 us
  Pallas kernels  53.7 us (93%)
  local copies, waits for them, and re-layouts  3.95 us (7%)
    pallas_call x1, Pallas kernels, body(): pl.pallas_call(kernel, out_shape=jax.ShapeDtypeStruct((5, 16, 4, 128), jn...  53.7 us
    unnamed x9, local copies, waits for them, and re-layouts  3.95 us

profile of v4, /device:TPU:1, one launch (start us, length us, event | category | flops | bytes accessed | tf_op | source)
XLA Modules:
  0.0 57.7 jit_solution(12416622607675077659)
XLA Ops:
  0.0 0.0 copy-start
  0.0 0.9 %copy-done = f32[5,16,4,128]{3,2,1,0:T(4,128)S(1)} copy-done((f32[5,16,4,128]{3,2,1,0:T(4,128)S(1)}, f32[5,16,4,128]{3,2,1,0:T(4,128)}, u32[]{:S(2)}) %copy-start) | copy-done | bytes 163864
  0.9 0.0 copy-start.1
  0.9 0.9 %copy-done.1 = f32[3,16,4,128]{3,2,1,0:T(4,128)S(1)} copy-done((f32[3,16,4,128]{3,2,1,0:T(4,128)S(1)}, f32[3,16,4,128]{3,2,1,0:T(4,128)}, u32[]{:S(2)}) %copy-start.1) | copy-done | bytes 98328
  1.8 0.0 copy-start.2
  1.8 0.8 %copy-done.2 = f32[16,4,128]{2,1,0:T(4,128)S(1)} copy-done((f32[16,4,128]{2,1,0:T(4,128)S(1)}, f32[16,4,128]{2,1,0:T(4,128)}, u32[]{:S(2)}) %copy-start.2) | copy-done | bytes 32792
  2.6 0.0 copy-start.3
  2.6 0.7 %copy-done.3 = f32[3,2,5,5]{3,1,2,0:T(2,128)S(1)} copy-done((f32[3,2,5,5]{3,1,2,0:T(2,128)S(1)}, f32[3,2,5,5]{3,1,2,0:T(2,128)}, u32[]{:S(2)}) %copy-start.3) | copy-done | bytes 624
  3.3 53.7 %shard_map.46 = f32[5,16,4,128]{3,2,1,0:T(4,128)S(1)} custom-call(f32[3,5,2,5]{3,2,1,0:T(2,128)S(1)} %bitcast.1, f32[5,16,4,128]{3,2,1,0:T(4,128)S(1)} %copy-done, f32[3,16,4,128]{3,2,1,0:T(4,128)S(1)} %copy-done.1, f32[16,4,128]{2,1,0:T(4,128)S(1)} %copy-done.2), custom_call_target="tpu_custom_call" | custom-call | flops 120000000 | bytes 600000 | tf_op jit(solution)/shard_map/pallas_call | solution.py:508
  57.0 0.7 %copy.6 = f32[5,16,4,128]{3,2,1,0:T(4,128)} copy(f32[5,16,4,128]{3,2,1,0:T(4,128)S(1)} %shard_map.46) | data formatting | bytes 327680
Async XLA Ops:
  0.0 0.9 %copy-start = (f32[5,16,4,128]{3,2,1,0:T(4,128)S(1)}, f32[5,16,4,128]{3,2,1,0:T(4,128)}, u32[]{:S(2)}) copy-start(f32[5,16,4,128]{3,2,1,0:T(4,128)} %explicit.1) | copy-start | bytes 491524
  0.9 0.9 %copy-start.1 = (f32[3,16,4,128]{3,2,1,0:T(4,128)S(1)}, f32[3,16,4,128]{3,2,1,0:T(4,128)}, u32[]{:S(2)}) copy-start(f32[3,16,4,128]{3,2,1,0:T(4,128)} %diffusion.1) | copy-start | bytes 294916
  1.8 0.8 %copy-start.2 = (f32[16,4,128]{2,1,0:T(4,128)S(1)}, f32[16,4,128]{2,1,0:T(4,128)}, u32[]{:S(2)}) copy-start(f32[16,4,128]{2,1,0:T(4,128)} %source_rate.1) | copy-start | bytes 98308
  2.6 0.7 %copy-start.3 = (f32[3,2,5,5]{3,1,2,0:T(2,128)S(1)}, f32[3,2,5,5]{3,1,2,0:T(2,128)}, u32[]{:S(2)}) copy-start(f32[3,2,5,5]{3,1,2,0:T(2,128)} %param.7) | copy-start | bytes 1804
